TPU v7x, 32 devices: a whole 2x2x4 slice. The times are simulated.
32 devices in a mesh: dp: 8 (over z, y), tensor: 4 (over x, core).
Axes of the slice: x: 2, y: 2, z: 4, core: 2. Of those that a mesh axis runs over, the one named last changes fastest.
Arguments:
- text_states: bfloat16 [8, 256, 4096], P('dp'), may hold values from -6 to 6
- prompt_lengths: int32 [8], P('dp'), may hold values from 1 to 256, as said below
- attn_gain: float32 [4096], replicated, may hold values from 0.1 to 1.9
- query_w: bfloat16 [4096, 2048], P('dp', 'tensor'), may hold values from -0.25 to 0.25
- key_w: bfloat16 [4096, 2048], P('dp', 'tensor'), may hold values from -0.25 to 0.25
- value_w: bfloat16 [4096, 2048], P('dp', 'tensor'), may hold values from -0.09375 to 0.09375
- out_w: bfloat16 [2048, 4096], P('tensor', 'dp'), may hold values from -0.125 to 0.125
- context_w: bfloat16 [4096, 2432], P('tensor', 'dp'), may hold values from -0.09375 to 0.09375
- mod_scale: float32 [8, 2432], P('dp'), may hold values from -0.5 to 0.5
- mod_shift: float32 [8, 2432], P('dp'), may hold values from -5 to 5
- text_key_w: bfloat16 [2432, 1536], P('dp', 'tensor'), may hold values from -0.125 to 0.125
- text_value_w: bfloat16 [2432, 1536], P('dp', 'tensor'), may hold values from -0.125 to 0.125
- image_query: bfloat16 [8, 512, 1536], P('dp', 'tensor'), may hold values from -30 to 30
- image_key: bfloat16 [8, 512, 1536], P('dp', 'tensor'), may hold values from -30 to 30
- image_value: bfloat16 [8, 512, 1536], P('dp', 'tensor'), may hold values from -6 to 6
Outputs:
- image_mixed: bfloat16 [8, 512, 1536], P('dp', 'tensor')
Inputs may be any that keep to these rules, and one draw needn't show every extreme that they name: `prompt_lengths`: some prompt has all 256 tokens in every draw.
All inputs are finite; a program needn't handle non-finite values.
Results may differ from a plain program's by a relative error of at most 0.015.
Values may be sent and summed in bfloat16 or wider, within the bound.
A program may use at most 64 MiB of HBM per device.

v0:
```python
import jax
import jax.numpy as jnp
from jax import lax
from jax.sharding import PartitionSpec as P

HEAD = 64


EPS = 1e-06


def rms_scale(values, gain):
    return values * lax.rsqrt(jnp.mean(values * values, axis=-1, keepdims=True) + EPS) * gain


def masked_softmax(scores, valid):
    scores = jnp.where(valid, scores, -jnp.inf)
    top = jnp.max(scores, axis=-1, keepdims=True)
    expo = jnp.exp(scores - top)
    return (expo, jnp.sum(expo, axis=-1, keepdims=True))


def joint_sample(items):
    query, keys, values, text_keys, text_values, text_ok = items
    nheads = query.shape[-1] // HEAD
    all_keys = jnp.concatenate([keys, text_keys], axis=0).reshape(-1, nheads, HEAD)
    all_values = jnp.concatenate([values, text_values], axis=0).reshape(-1, nheads, HEAD)
    slot_ok = jnp.concatenate([lax.iota(jnp.int32, keys.shape[0]) >= 0, text_ok])
    scores = jnp.einsum(
        "qhd,khd->hqk",
        query.reshape(-1, nheads, HEAD),
        all_keys,
        preferred_element_type=jnp.float32,
    ) * HEAD ** (-0.5)
    expo, total = masked_softmax(scores, slot_ok[None, None, :])
    result = jnp.einsum(
        "hqk,khd->qhd", expo.astype(jnp.bfloat16), all_values, preferred_element_type=jnp.float32
    )
    result = result / jnp.swapaxes(total, 0, 1)
    return result.astype(jnp.bfloat16).reshape(query.shape[0], -1)


def per_device(
    text_states,
    prompt_lengths,
    attn_gain,
    query_w,
    key_w,
    value_w,
    out_w,
    context_w,
    mod_scale,
    mod_shift,
    text_key_w,
    text_value_w,
    image_query,
    image_key,
    image_value,
):
    prompts, slots, enc = text_states.shape
    flat = text_states.astype(jnp.float32).reshape(prompts * slots, enc)
    normed = rms_scale(flat, attn_gain).astype(jnp.bfloat16)
    local_width = query_w.shape[1]
    pieces = (
        lax.all_gather(query_w, "dp", axis=0, tiled=True),
        lax.all_gather(key_w, "dp", axis=0, tiled=True),
        lax.all_gather(value_w, "dp", axis=0, tiled=True),
    )
    columns = normed
    enc_q, enc_k, enc_v = tuple(
        (jnp.dot(columns, piece, preferred_element_type=jnp.float32) for piece in pieces)
    )
    heads_here = local_width // HEAD

    def split_heads(values):
        return values.astype(jnp.bfloat16).reshape(prompts, slots, heads_here, HEAD)

    enc_q = split_heads(enc_q)
    enc_k = split_heads(enc_k)
    enc_v = split_heads(enc_v)
    text_ok = lax.iota(jnp.int32, slots)[None, :] < prompt_lengths[:, None]
    scores = jnp.einsum("bqhd,bkhd->bhqk", enc_q, enc_k, preferred_element_type=jnp.float32)
    expo, total = masked_softmax(scores, text_ok[:, None, None, :])
    mixed = jnp.einsum(
        "bhqk,bkhd->bqhd", expo.astype(jnp.bfloat16), enc_v, preferred_element_type=jnp.float32
    )
    mixed = (
        (mixed / jnp.swapaxes(total, 1, 2))
        .astype(jnp.bfloat16)
        .reshape(prompts * slots, local_width)
    )
    partial_value = jnp.dot(
        mixed, lax.all_gather(out_w, "dp", axis=1, tiled=True), preferred_element_type=jnp.float32
    )
    share_width = context_w.shape[0]
    offset = lax.axis_index("tensor") * share_width
    summed = flat + lax.psum(partial_value.astype(jnp.bfloat16), "tensor").astype(jnp.float32)
    embedded = lax.dynamic_slice_in_dim(summed, offset, share_width, 1).astype(jnp.bfloat16)
    context_part = jnp.dot(
        embedded,
        lax.all_gather(context_w, "dp", axis=1, tiled=True),
        preferred_element_type=jnp.float32,
    )
    context = (
        lax.psum(context_part.astype(jnp.bfloat16), "tensor")
        .astype(jnp.float32)
        .reshape(prompts, slots, -1)
    )
    centered = context - jnp.mean(context, axis=-1, keepdims=True)
    spread = jnp.mean(centered * centered, axis=-1, keepdims=True)
    modulated = (
        centered * lax.rsqrt(spread + EPS) * (1.0 + mod_scale[:, None, :]) + mod_shift[:, None, :]
    )
    modulated = modulated.astype(jnp.bfloat16).reshape(prompts * slots, -1)
    text_width = text_key_w.shape[1]
    pieces = (
        lax.all_gather(text_key_w, "dp", axis=0, tiled=True),
        lax.all_gather(text_value_w, "dp", axis=0, tiled=True),
    )
    columns = modulated
    text_keys = jnp.dot(columns, pieces[0], preferred_element_type=jnp.float32)
    text_values = jnp.dot(columns, pieces[1], preferred_element_type=jnp.float32)
    text_keys = text_keys.astype(jnp.bfloat16).reshape(prompts, slots, text_width)
    text_values = text_values.astype(jnp.bfloat16).reshape(prompts, slots, text_width)
    by_head = (
        lax.all_to_all(image_query, "tensor", split_axis=2, concat_axis=1, tiled=True),
        lax.all_to_all(image_key, "tensor", split_axis=2, concat_axis=1, tiled=True),
        lax.all_to_all(image_value, "tensor", split_axis=2, concat_axis=1, tiled=True),
    )
    attended = lax.map(
        joint_sample, (by_head[0], by_head[1], by_head[2], text_keys, text_values, text_ok)
    )
    return lax.all_to_all(attended, "tensor", split_axis=1, concat_axis=2, tiled=True)


def solution(mesh):
    in_specs = (
        P("dp", None, None),
        P("dp"),
        P(),
        P("dp", "tensor"),
        P("dp", "tensor"),
        P("dp", "tensor"),
        P("tensor", "dp"),
        P("tensor", "dp"),
        P("dp", None),
        P("dp", None),
        P("dp", "tensor"),
        P("dp", "tensor"),
        P("dp", "tensor", None),
        P("dp", "tensor", None),
        P("dp", "tensor", None),
    )
    out_specs = P("dp", "tensor", None)
    return jax.shard_map(
        per_device, mesh=mesh, in_specs=in_specs, out_specs=out_specs, check_vma=False
    )
```

profile of v0, /device:TPU:1, one launch (start us, length us, event | category | flops | bytes accessed | tf_op | source)
XLA Modules:
  0.0 622.8 jit_solution(11414756756488963756)
XLA Ops:
  6.5 0.7 all-gather.10.cloned.1.call-update
  7.3 0.7 all-gather.12.cloned.1.call-update
  8.1 0.7 all-gather.8.cloned.1.call-update
  8.8 0.5 all-gather.14.cloned.1.call-update
  10.0 0.5 multiply_reduce_fusion
  10.5 73.3 %all-gather.10.cloned.1.call-done = bf16[4096,512]{1,0:T(8,128)(2,1)} async-done(((bf16[512,512]{1,0:T(8,128)(2,1)}), bf16[4096,512]{1,0:T(8,128)(2,1)}) %all-gather.10.cloned.1.call-update) | async-done | bytes 4194320 | tf_op jit(solution)/shard_map/all_gather | solution.py:65
  83.8 3.5 convolution_convert_fusion.3
  87.5 70.2 %all-gather.12.cloned.1.call-done = bf16[4096,512]{1,0:T(8,128)(2,1)} async-done(((bf16[512,512]{1,0:T(8,128)(2,1)}), bf16[4096,512]{1,0:T(8,128)(2,1)}) %all-gather.12.cloned.1.call-update) | async-done | bytes 4194320 | tf_op jit(solution)/shard_map/all_gather | solution.py:66
  157.6 3.5 convolution_convert_fusion.2
  161.3 70.2 %all-gather.8.cloned.1.call-done = bf16[4096,512]{1,0:T(8,128)(2,1)} async-done(((bf16[512,512]{1,0:T(8,128)(2,1)}), bf16[4096,512]{1,0:T(8,128)(2,1)}) %all-gather.8.cloned.1.call-update) | async-done | bytes 4194320 | tf_op jit(solution)/shard_map/all_gather | solution.py:67
  231.5 3.5 convolution_convert_fusion.4
  235.1 0.5 select_reduce_fusion
  235.6 0.4 fusion.12
  236.1 0.6 fusion.18
  236.6 70.8 %all-gather.14.cloned.1.call-done = bf16[512,4096]{1,0:T(8,128)(2,1)} async-done(((bf16[512,512]{1,0:T(8,128)(2,1)}), bf16[512,4096]{1,0:T(8,128)(2,1)}) %all-gather.14.cloned.1.call-update) | async-done | bytes 4194320 | tf_op jit(solution)/shard_map/all_gather | solution.py:93
  307.4 4.9 convolution_convert_fusion
  312.4 0.5 all-gather.16.cloned.1.call-update
  313.0 2.5 bitcast_convert_fusion
  315.5 46.9 %all-reduce.4.cloned.1.call-done = bf16[256,4096]{1,0:T(8,128)(2,1)} async-done(((bf16[256,4096]{1,0:T(8,128)(2,1)}), bf16[256,4096]{1,0:T(8,128)(2,1)}) %all-reduce.4.cloned.1.call-update) | async-done | bytes 2097168 | tf_op jit(solution)/shard_map/psum | solution.py:97
  362.4 84.6 %all-gather.16.cloned.1.call-done = bf16[1024,2432]{0,1:T(8,128)(2,1)} async-done(((bf16[1024,304]{0,1:T(8,128)(2,1)}), bf16[1024,2432]{0,1:T(8,128)(2,1)}) %all-gather.16.cloned.1.call-update) | async-done | bytes 4980752 | tf_op jit(solution)/shard_map/all_gather | solution.py:101
  447.0 5.5 convolution_convert_fusion.1
  452.6 0.7 all-gather.20.cloned.1.call-update
  453.3 0.2 all-gather.18.cloned.1.call-start
  453.5 0.5 all-gather.18.cloned.1.call-update
  454.0 0.6 copy.74
  454.6 0.5 broadcast.94
  455.1 8.7 %reduce.12 = bf16[1536,128]{1,0:T(8,128)(2,1)S(1)} reduce(bf16[1536,1,128]{2,1,0:T(2,128)(2,1)S(1)} %bitcast.96, bf16[]{:T(256)} %broadcast.94), dimensions={1}, to_apply=%bitcast.77.reduce_sub_computation | reduce | bytes 786434
  463.9 0.8 reshape.149
  464.7 5.2 all-to-all-start.1
  469.9 0.6 copy.77
  470.5 8.7 %reduce.11 = bf16[1536,128]{1,0:T(8,128)(2,1)S(1)} reduce(bf16[1536,1,128]{2,1,0:T(2,128)(2,1)S(1)} %bitcast.102, bf16[]{:T(256)} %broadcast.94), dimensions={1}, to_apply=%bitcast.75.reduce_sub_computation | reduce | bytes 786434
  479.2 0.8 reshape.147
  480.1 3.6 all-to-all-start.2
  483.7 0.6 copy.67
  484.2 8.7 %reduce.13 = bf16[1536,128]{1,0:T(8,128)(2,1)S(1)} reduce(bf16[1536,1,128]{2,1,0:T(2,128)(2,1)S(1)} %bitcast.103, bf16[]{:T(256)} %broadcast.94), dimensions={1}, to_apply=%bitcast.79.reduce_sub_computation | reduce | bytes 786434
  493.0 0.8 reshape.151
  493.8 0.8 all-to-all-done.2
  494.6 3.9 all-to-all-start
  498.6 0.4 reshape.150
  499.1 0.3 copy.75
  499.4 0.2 concatenate.26
  499.5 0.4 reshape.148
  500.0 0.3 copy.78
  500.3 0.2 reshape.142
  500.5 4.5 all-to-all-done
  505.1 0.4 reshape.152
  505.5 0.3 copy.68
  505.8 0.2 concatenate.22
  506.0 1.6 convert_reduce_fusion
  507.7 1.8 fusion.8
  509.5 33.1 %all-gather.20.cloned.1.call-done = bf16[2432,384]{1,0:T(8,128)(2,1)} async-done(((bf16[304,384]{1,0:T(8,128)(2,1)}), bf16[2432,384]{1,0:T(8,128)(2,1)}) %all-gather.20.cloned.1.call-update) | async-done | bytes 1867792 | tf_op jit(solution)/shard_map/all_gather | solution.py:117
  542.5 2.4 convolution_convert_fusion.5
  545.1 45.3 %all-gather.18.cloned.1.call-done = bf16[2432,384]{1,0:T(8,128)(2,1)} async-done(((bf16[304,384]{1,0:T(8,128)(2,1)}), bf16[2432,384]{1,0:T(8,128)(2,1)}) %all-gather.18.cloned.1.call-update) | async-done | bytes 1867792 | tf_op jit(solution)/shard_map/all_gather | solution.py:118
  590.3 2.4 convolution_convert_fusion.6
  592.7 0.1 copy.73
  592.9 2.2 bitcast_reduce_fusion
  595.0 2.3 fusion.1
  597.4 2.2 fusion.27
  599.6 1.4 copy.80
  600.9 2.9 reduce.14
  604.0 10.7 %all_to_all.63 = bf16[4,2,24576]{2,1,0:T(2,128)(2,1)S(1)} all-to-all(bf16[4,2,24576]{2,1,0:T(2,128)(2,1)S(1)} %reshape.153), channel_id=1, replica_groups=mesh['dp'=8,'tensor'=4] {'tensor'}, dimensions={0} | all-to-all | bytes 786432 | tf_op jit(solution)/shard_map/all_to_all | solution.py:133
  614.6 0.4 reshape.154
  615.1 0.2 copy.81
  615.3 0.9 copy.82
  (44 shorter events, 1.3 us)
Async XLA Ops:
  6.5 3.5 copy-start
  6.5 77.3 %copy-start.7 = (f32[4096]{0:T(1024)S(1)}, f32[4096]{0:T(1024)}, u32[]{:S(2)}) copy-start(f32[4096]{0:T(1024)} %param.17) | copy-start | bytes 49156
  6.5 77.3 %all-gather.10.cloned.1.call-start = ((), (), s32[]{:S(2)}) async-start(), calls=%async_computation.5 | async-start | bytes 4718592 | tf_op jit(solution)/shard_map/all_gather | solution.py:65
  7.3 150.4 %all-gather.12.cloned.1.call-start = ((), (), s32[]{:S(2)}) async-start(), calls=%async_computation.6 | async-start | bytes 4718592 | tf_op jit(solution)/shard_map/all_gather | solution.py:66
  8.0 223.5 %all-gather.8.cloned.1.call-start = ((), (), s32[]{:S(2)}) async-start(), calls=%async_computation.4 | async-start | bytes 4718592 | tf_op jit(solution)/shard_map/all_gather | solution.py:67
  8.7 298.7 %all-gather.14.cloned.1.call-start = ((), (), s32[]{:S(2)}) async-start(), calls=%async_computation.7 | async-start | bytes 4718592 | tf_op jit(solution)/shard_map/all_gather | solution.py:93
  9.3 353.1 %all-reduce.4.cloned.1.call-start = ((), (), s32[]{:S(2)}) async-start(), calls=%async_computation.8 | async-start | bytes 4194304 | tf_op jit(solution)/shard_map/psum | solution.py:97
  312.3 134.6 %all-gather.16.cloned.1.call-start = ((), (), s32[]{:S(2)}) async-start(), calls=%async_computation.9 | async-start | bytes 5603328 | tf_op jit(solution)/shard_map/all_gather | solution.py:101
  312.9 193.1 %all-reduce.6.cloned.1.call-start = ((), (), s32[]{:S(2)}) async-start(), calls=%async_computation.10 | async-start | bytes 2490368 | tf_op jit(solution)/shard_map/psum | solution.py:105
  315.5 138.5 %copy-start.2 = (bf16[1,128,1536]{2,1,0:T(8,128)(2,1)S(1)}, bf16[1,128,1536]{2,1,0:T(8,128)(2,1)}, u32[]{:S(2)}) copy-start(bf16[1,128,1536]{2,1,0:T(8,128)(2,1)} %param.28) | copy-start | bytes 1179652
  452.5 17.4 %copy-start.3 = (bf16[1,128,1536]{2,1,0:T(8,128)(2,1)S(1)}, bf16[1,128,1536]{2,1,0:T(8,128)(2,1)}, u32[]{:S(2)}) copy-start(bf16[1,128,1536]{2,1,0:T(8,128)(2,1)} %param.27) | copy-start | bytes 1179652
  452.5 90.0 %all-gather.20.cloned.1.call-start = ((), (), s32[]{:S(2)}) async-start(), calls=%async_computation.12 | async-start | bytes 2101248 | tf_op jit(solution)/shard_map/all_gather | solution.py:117
  453.3 137.0 %all-gather.18.cloned.1.call-start = ((), (), s32[]{:S(2)}) async-start(), calls=%async_computation.11 | async-start | bytes 2101248 | tf_op jit(solution)/shard_map/all_gather | solution.py:118
  464.7 19.0 %copy-start.4 = (bf16[1,128,1536]{2,1,0:T(8,128)(2,1)S(1)}, bf16[1,128,1536]{2,1,0:T(8,128)(2,1)}, u32[]{:S(2)}) copy-start(bf16[1,128,1536]{2,1,0:T(8,128)(2,1)} %param.29) | copy-start | bytes 1179652
  464.7 15.3 %all-to-all-start.1 = ((bf16[4,2,24576]{2,1,0:T(2,128)(2,1)}), bf16[4,2,24576]{2,1,0:T(2,128)(2,1)S(1)}, u32[]{:S(2)}, u32[]{:S(2)}) async-start(bf16[4,2,24576]{2,1,0:T(2,128)(2,1)} %reshape.149), calls=%async_computation.1 | async-start | bytes 786432 | tf_op jit(solution)/shard_map/all_to_all | solution.py:127
  480.0 18.4 %copy-start.5 = (f32[1,2432]{1,0:T(1,128)S(1)}, f32[1,2432]{1,0:T(1,128)}, u32[]{:S(2)}) copy-start(f32[1,2432]{1,0:T(1,128)} %param.24) | copy-start | bytes 29188
  480.0 18.5 %copy-start.6 = (f32[1,2432]{1,0:T(1,128)S(1)}, f32[1,2432]{1,0:T(1,128)}, u32[]{:S(2)}) copy-start(f32[1,2432]{1,0:T(1,128)} %param.23) | copy-start | bytes 29188
  480.1 14.5 %all-to-all-start.2 = ((bf16[4,2,24576]{2,1,0:T(2,128)(2,1)}), bf16[4,2,24576]{2,1,0:T(2,128)(2,1)S(1)}, u32[]{:S(2)}, u32[]{:S(2)}) async-start(bf16[4,2,24576]{2,1,0:T(2,128)(2,1)} %reshape.147), calls=%async_computation.2 | async-start | bytes 786432 | tf_op jit(solution)/shard_map/all_to_all | solution.py:126
  494.6 10.5 %all-to-all-start = ((bf16[4,2,24576]{2,1,0:T(2,128)(2,1)}), bf16[4,2,24576]{2,1,0:T(2,128)(2,1)S(1)}, u32[]{:S(2)}, u32[]{:S(2)}) async-start(bf16[4,2,24576]{2,1,0:T(2,128)(2,1)} %reshape.151), calls=%async_computation | async-start | bytes 786432 | tf_op jit(solution)/shard_map/all_to_all | solution.py:128
  506.0 36.5 %copy-start.1 = (bf16[256,2432]{1,0:T(8,128)(2,1)S(1)}, bf16[256,2432]{1,0:T(8,128)(2,1)}, u32[]{:S(2)}) copy-start(bf16[256,2432]{1,0:T(8,128)(2,1)} %all-reduce.6.cloned.1.call-done) | copy-start | bytes 3735556
Sparse Core Ops, SparseCore 0:
  9.5 74.2 all-gather.9
  85.9 71.6 all-gather.11
  159.8 71.6 all-gather.7
  233.4 74.0 all-gather.13
  312.5 49.8 all-reduce.3
  364.7 82.2 all-gather.15
  452.6 41.3 all-reduce.5
  496.2 46.3 all-gather.19
  544.7 45.5 all-gather.17
where the time goes:
time: 624 us; the launch traced here: 623 us
  waiting for transfers between devices  504 us (81%)
  other arithmetic  38.4 us (6%)
  matrix products  31.1 us (5%)
  between operations  14.2 us (2%)
  starting transfers between devices  13.2 us (2%)
  local copies, waits for them, and re-layouts  11.4 us (2%)
  blocking collectives  10.7 us (2%)
    all_gather x1, waiting for transfers between devices, per_device(): lax.all_gather(context_w, 'dp', axis=1, tiled=True)  84.6 us
    all_gather x1, waiting for transfers between devices, per_device(): lax.all_gather(query_w, 'dp', axis=0, tiled=True)  73.3 us
    all_gather x1, waiting for transfers between devices, per_device(): lax.all_gather(out_w, 'dp', axis=1, tiled=True)  70.8 us
    all_gather x1, waiting for transfers between devices, per_device(): lax.all_gather(value_w, 'dp', axis=0, tiled=True)  70.2 us
    all_gather x1, waiting for transfers between devices, per_device(): lax.all_gather(key_w, 'dp', axis=0, tiled=True)  70.2 us
    psum x1, waiting for transfers between devices, per_device(): lax.psum(partial_value.astype(jnp.bfloat16), 'tensor').astype(jnp.float32)  46.9 us
    all_gather x1, waiting for transfers between devices, per_device(): lax.all_gather(text_value_w, 'dp', axis=0, tiled=True)  45.3 us
    all_gather x1, waiting for transfers between devices, per_device(): lax.all_gather(text_key_w, 'dp', axis=0, tiled=True)  33.1 us
  transfers between devices with their start and end apart: 12, of which 10 were waited for; matrix products, arithmetic and copies ran while one was open for 9% of the time, Pallas kernels for 0%

commit v1 on v0

v1 whole, which is shorter than its diff:
```python
import functools

import jax
import jax.numpy as jnp
from jax import lax
from jax.experimental import pallas as pl
from jax.experimental.pallas import tpu as pltpu
from jax.sharding import PartitionSpec as P

HEAD = 64
EPS = 1e-06
MESH = pl.DeviceIdType.MESH
F32 = jnp.float32
BF16 = jnp.bfloat16


def split_rows(rows, count):
    if rows % 16:
        return [(0, rows)]
    size = -(-rows // (count * 16)) * 16
    return [(i * size, min(size, rows - i * size)) for i in range(count)]


def kernel(n, nt, *refs):
    (
        len_ref, x_ref, gain_ref, scale_ref, shift_ref,
        q_in, k_in, v_in, o_in, c_in, tk_in, tv_in, iq_in, ik_in, iv_in,
        out_ref,
        wq, wk, wv, wo, wc, wtk, wtv,
        normed, eq, ek, ev, mixed, part, part_in, emb, ctx, ctx_in, mod,
        iq, ik, iv, tk, tv, att,
        own_sem, ring_send, ring_recv, img_send, img_recv, img_own,
        part_send, part_recv, ctx_send, ctx_recv, mod_send, mod_recv,
        att_send, att_recv, att_own,
    ) = refs
    d = lax.axis_index("dp")
    t = lax.axis_index("tensor")
    half = n // 2

    def device_at(place):
        back = place // half
        return 2 * (place * (1 - back) + (n - 1 - place) * back) + back

    odd = d % 2
    place = (d // 2) * (1 - odd) + (n - 1 - d // 2) * odd
    right = device_at((place + 1) % n)
    left = device_at((place + n - 1) % n)
    peers = [(t + k) % nt for k in range(1, nt)]

    barrier = pltpu.get_barrier_semaphore()
    for neighbour in (left, right):
        pl.semaphore_signal(barrier, inc=1, device_id=(neighbour, t), device_id_type=MESH)
    for peer in peers:
        pl.semaphore_signal(barrier, inc=1, device_id=(d, peer), device_id_type=MESH)

    weights = [(q_in, wq), (k_in, wk), (v_in, wv), (o_in, wo), (c_in, wc), (tk_in, wtk), (tv_in, wtv)]
    own = [
        pltpu.make_async_copy(src, dst.at[d], own_sem.at[i])
        for i, (src, dst) in enumerate(weights)
    ]
    for copy in own:
        copy.start()
    pl.semaphore_wait(barrier, 2 + nt - 1)

    chunks = []

    def add(weight, index, runs, forward):
        made = []
        for run in runs:
            made.append((len(chunks), weight, run, forward))
            chunks.append(made[-1])
        return made

    def hop(chunk, step, incoming=False):
        number, weight, (start, size), forward = chunk
        back = step + 1 if incoming else step
        owner = device_at((place - back + n) % n if forward else (place + back) % n)
        view = weight.at[owner, pl.ds(start, size)] if size < weight.shape[1] else weight.at[owner]
        return pltpu.make_async_remote_copy(
            src_ref=view, dst_ref=view,
            send_sem=ring_send.at[number], recv_sem=ring_recv.at[number, step],
            device_id=(right if forward else left, t), device_id_type=MESH,
        )

    def open_ring(group):
        for chunk in group:
            hop(chunk, 0).start()

    def run_ring(group, first, last):
        @pl.loop(first, last)
        def _(step):
            for chunk in group:
                hop(chunk, step - 1, incoming=True).wait_recv()
                hop(chunk, step - 1).wait_send()
                hop(chunk, step).start()

    def close_ring(group):
        for chunk in group:
            hop(chunk, n - 2, incoming=True).wait_recv()
            hop(chunk, n - 2).wait_send()

    rows = q_in.shape[0]
    group_qk = add(wq, 0, split_rows(rows, 2), True) + add(wk, 1, split_rows(rows, 2), False)
    group_vo = add(wv, 2, split_rows(rows, 2), True) + add(wo, 3, split_rows(o_in.shape[0], 2), False)
    quarters = split_rows(c_in.shape[0], 4)
    group_c = add(wc, 4, quarters[:2], True) + add(wc, 4, quarters[2:], False)
    trows = tk_in.shape[0]
    group_t = add(wtk, 5, split_rows(trows, 2), True) + add(wtv, 6, split_rows(trows, 2), False)

    own[0].wait()
    own[1].wait()
    open_ring(group_qk)

    lat, cols = iq.shape[1:]

    def columns_of(ref, who):
        if len(ref.shape) == 3:
            return ref.at[who]
        return ref.at[:, pl.ds(pl.multiple_of(who * cols, 128), cols)]

    def image_copy(a, src, dst, peer, place_of):
        return pltpu.make_async_remote_copy(
            src_ref=columns_of(src, peer),
            dst_ref=dst.at[place_of],
            send_sem=img_send.at[a, peer], recv_sem=img_recv.at[a, place_of],
            device_id=(d, peer), device_id_type=MESH,
        )

    images = [(iq_in, iq), (ik_in, ik), (iv_in, iv)]
    image_own = []
    for a, (src, dst) in enumerate(images):
        copy = pltpu.make_async_copy(
            columns_of(src, t), dst.at[t], img_own.at[a]
        )
        copy.start()
        image_own.append(copy)
        for peer in peers:
            image_copy(a, src, dst, peer, t).start()

    for copy in own[2:]:
        copy.wait()

    slots, enc = x_ref.shape
    length = len_ref[0]

    @pl.loop(0, slots // 32)
    def _(i):
        block = pl.ds(pl.multiple_of(i * 32, 32), 32)
        x = x_ref[block, :].astype(F32)
        scale = lax.rsqrt(jnp.mean(x * x, axis=-1, keepdims=True) + EPS)
        normed[block, :] = (x * scale * gain_ref[...]).astype(BF16)

    width = q_in.shape[1]

    def project(weight, result):
        @pl.loop(0, width // 256)
        def _(j):
            block = pl.ds(pl.multiple_of(j * 256, 256), 256)
            w = weight[:, :, block].reshape(enc, 256)
            result[:, block] = jnp.dot(normed[...], w, preferred_element_type=F32).astype(BF16)

    run_ring(group_qk, 1, n - 1)
    open_ring(group_vo)
    close_ring(group_qk)
    project(wq, eq)
    project(wk, ek)

    run_ring(group_vo, 1, n - 1)
    open_ring(group_c)
    open_ring(group_t)
    close_ring(group_vo)
    project(wv, ev)

    for h in range(width // HEAD):
        at = slice(h * HEAD, (h + 1) * HEAD)
        scores = lax.dot_general(
            eq[:, at], ek[:, at], (((1,), (1,)), ((), ())), preferred_element_type=F32
        )
        valid = lax.broadcasted_iota(jnp.int32, scores.shape, 1) < length
        scores = jnp.where(valid, scores, -jnp.inf)
        expo = jnp.exp(scores - jnp.max(scores, axis=-1, keepdims=True))
        total = jnp.sum(expo, axis=-1, keepdims=True)
        value = jnp.dot(expo.astype(BF16), ev[:, at], preferred_element_type=F32)
        mixed[:, at] = (value / total).astype(BF16)

    ocols = o_in.shape[1]
    share = enc // nt
    per = share // ocols

    @pl.loop(0, n)
    def _(j):
        value = jnp.dot(mixed[...], wo[j], preferred_element_type=F32).astype(BF16)
        part[j // per, :, pl.ds(pl.multiple_of((j % per) * ocols, 128), ocols)] = value

    def part_copy(peer, place_of):
        return pltpu.make_async_remote_copy(
            src_ref=part.at[peer], dst_ref=part_in.at[place_of],
            send_sem=part_send.at[peer], recv_sem=part_recv.at[place_of],
            device_id=(d, peer), device_id_type=MESH,
        )

    for peer in peers:
        part_copy(peer, t).start()
    run_ring(group_c, 1, n - 1)
    for peer in peers:
        part_copy(peer, peer).wait_recv()

    @pl.loop(0, slots // 32)
    def _(i):
        block = pl.ds(pl.multiple_of(i * 32, 32), 32)
        total = part[t, block, :].astype(F32)
        for peer in peers:
            total = total + part_in[peer, block, :].astype(F32)
        x = x_ref[block, pl.ds(pl.multiple_of(t * share, 128), share)].astype(F32)
        emb[block, :] = (x + total).astype(BF16)

    close_ring(group_c)

    @pl.loop(0, n)
    def _(j):
        ctx[j] = jnp.dot(emb[...], wc[j], preferred_element_type=F32).astype(BF16)

    trow = slots // nt

    def token_rows(who):
        return pl.ds(pl.multiple_of(who * trow, 16), trow)

    def ctx_copy(peer, place_of):
        return pltpu.make_async_remote_copy(
            src_ref=ctx.at[:, token_rows(peer)], dst_ref=ctx_in.at[place_of],
            send_sem=ctx_send.at[peer], recv_sem=ctx_recv.at[place_of],
            device_id=(d, peer), device_id_type=MESH,
        )

    for peer in peers:
        ctx_copy(peer, t).start()
    middle = 1 + (n - 1) // 3
    run_ring(group_t, 1, middle)
    for peer in peers:
        ctx_copy(peer, peer).wait_recv()
    context = ctx[:, token_rows(t), :].astype(F32)
    for peer in peers:
        context = context + ctx_in[peer].astype(F32)
    features = context.shape[0] * context.shape[2]

    def mean(values):
        return jnp.sum(jnp.sum(values, axis=0), axis=-1, keepdims=True)[None] / features

    centered = context - mean(context)
    spread = mean(centered * centered)
    modulated = centered * lax.rsqrt(spread + EPS) * (1.0 + scale_ref[...]) + shift_ref[...]
    mod[:, token_rows(t), :] = modulated.astype(BF16)

    def mod_copy(peer, place_of):
        view = mod.at[:, token_rows(place_of)]
        return pltpu.make_async_remote_copy(
            src_ref=view, dst_ref=view,
            send_sem=mod_send.at[peer], recv_sem=mod_recv.at[place_of],
            device_id=(d, peer), device_id_type=MESH,
        )

    for peer in peers:
        mod_copy(peer, t).start()
    run_ring(group_t, middle, n - 1)
    for a, (src, dst) in enumerate(images):
        image_own[a].wait()
        for peer in peers:
            image_copy(a, src, dst, peer, peer).wait_recv()
    for peer in peers:
        mod_copy(peer, peer).wait_recv()
    close_ring(group_t)

    def text_project(weight, result):
        total = jnp.dot(mod[0], weight[0], preferred_element_type=F32)
        for j in range(1, n):
            total = total + jnp.dot(mod[j], weight[j], preferred_element_type=F32)
        result[...] = total.astype(BF16)

    text_project(wtk, tk)
    text_project(wtv, tv)

    for h in range(cols // HEAD):
        at = slice(h * HEAD, (h + 1) * HEAD)
        keys = ik[:, :, at].reshape(nt * lat, HEAD)
        values = iv[:, :, at].reshape(nt * lat, HEAD)
        queries = iq[:, :, at].reshape(nt * lat, HEAD)
        score = functools.partial(
            lax.dot_general, dimension_numbers=(((1,), (1,)), ((), ())), preferred_element_type=F32
        )
        first = score(queries, keys) * HEAD ** (-0.5)
        second = score(queries, tk[:, at]) * HEAD ** (-0.5)
        valid = lax.broadcasted_iota(jnp.int32, second.shape, 1) < length
        second = jnp.where(valid, second, -jnp.inf)
        top = jnp.maximum(
            jnp.max(first, axis=-1, keepdims=True), jnp.max(second, axis=-1, keepdims=True)
        )
        first = jnp.exp(first - top)
        second = jnp.exp(second - top)
        total = jnp.sum(first, axis=-1, keepdims=True) + jnp.sum(second, axis=-1, keepdims=True)
        value = jnp.dot(first.astype(BF16), values, preferred_element_type=F32)
        value = value + jnp.dot(second.astype(BF16), tv[:, at], preferred_element_type=F32)
        att[:, :, at] = (value / total).astype(BF16).reshape(nt, lat, HEAD)

    def att_copy(peer, place_of):
        return pltpu.make_async_remote_copy(
            src_ref=att.at[peer], dst_ref=columns_of(out_ref, place_of),
            send_sem=att_send.at[peer], recv_sem=att_recv.at[place_of],
            device_id=(d, peer), device_id_type=MESH,
        )

    for peer in peers:
        att_copy(peer, t).start()
    copy = pltpu.make_async_copy(att.at[t], columns_of(out_ref, t), att_own)
    copy.start()
    copy.wait()
    for peer in peers:
        for a, (src, dst) in enumerate(images):
            image_copy(a, src, dst, peer, t).wait_send()
        part_copy(peer, t).wait_send()
        ctx_copy(peer, t).wait_send()
        mod_copy(peer, t).wait_send()
        att_copy(peer, t).wait_send()
    for peer in peers:
        att_copy(peer, peer).wait_recv()


def per_device(
    n, nt,
    text_states, prompt_lengths, attn_gain, query_w, key_w, value_w, out_w, context_w,
    mod_scale, mod_shift, text_key_w, text_value_w, image_query, image_key, image_value,
):
    prompts, slots, enc = text_states.shape
    lat, joint = image_query.shape[1:]
    width = query_w.shape[1]
    cols = joint // nt
    ccols = context_w.shape[1]
    vmem = pl.BlockSpec(memory_space=pltpu.VMEM)
    anywhere = pl.BlockSpec(memory_space=pl.ANY)
    dma = pltpu.SemaphoreType.DMA
    scratch = [pltpu.VMEM((n,) + w.shape, BF16) for w in (query_w, key_w, value_w, out_w, context_w, text_key_w, text_value_w)]
    scratch += [
        pltpu.VMEM((slots, enc), BF16),
        pltpu.VMEM((slots, width), BF16),
        pltpu.VMEM((slots, width), BF16),
        pltpu.VMEM((slots, width), BF16),
        pltpu.VMEM((slots, width), BF16),
        pltpu.VMEM((nt, slots, enc // nt), BF16),
        pltpu.VMEM((nt, slots, enc // nt), BF16),
        pltpu.VMEM((slots, enc // nt), BF16),
        pltpu.VMEM((n, slots, ccols), BF16),
        pltpu.VMEM((nt, n, slots // nt, ccols), BF16),
        pltpu.VMEM((n, slots, ccols), BF16),
        pltpu.VMEM((nt, lat, cols), BF16),
        pltpu.VMEM((nt, lat, cols), BF16),
        pltpu.VMEM((nt, lat, cols), BF16),
        pltpu.VMEM((slots, cols), BF16),
        pltpu.VMEM((slots, cols), BF16),
        pltpu.VMEM((nt, lat, cols), BF16),
        dma((7,)), dma((16,)), dma((16, n - 1)),
        dma((3, nt)), dma((3, nt)), dma((3,)),
        dma((nt,)), dma((nt,)), dma((nt,)), dma((nt,)), dma((nt,)), dma((nt,)),
        dma((nt,)), dma((nt,)), dma,
    ]
    flops = 2 * slots * (enc * width * 4 + enc // nt * ccols * n + ccols * n * cols * 2) + 4 * lat * nt * (lat * nt + slots) * cols
    apart = cols % 128 != 0

    def laid_out(array):
        array = array.reshape(lat, joint)
        return array.reshape(lat, nt, cols).swapaxes(0, 1) if apart else array

    result = pl.pallas_call(
        functools.partial(kernel, n, nt),
        out_shape=jax.ShapeDtypeStruct((nt, lat, cols) if apart else (lat, joint), BF16),
        in_specs=[pl.BlockSpec(memory_space=pltpu.SMEM)] + [vmem] * 4 + [anywhere] * 10,
        out_specs=vmem,
        scratch_shapes=scratch,
        compiler_params=pltpu.CompilerParams(
            collective_id=0, has_side_effects=True, vmem_limit_bytes=60 * 2**20
        ),
        cost_estimate=pl.CostEstimate(flops=flops, bytes_accessed=12 * 2**20, transcendentals=3 * 2**20),
    )(
        prompt_lengths,
        text_states.reshape(slots, enc),
        attn_gain.reshape(1, enc),
        mod_scale.reshape(n, 1, ccols),
        mod_shift.reshape(n, 1, ccols),
        query_w, key_w, value_w, out_w, context_w, text_key_w, text_value_w,
        laid_out(image_query), laid_out(image_key), laid_out(image_value),
    )
    if apart:
        result = result.swapaxes(0, 1)
    return result.reshape(1, lat, joint)


def solution(mesh):
    n, nt = mesh.shape["dp"], mesh.shape["tensor"]
    in_specs = (
        P("dp", None, None),
        P("dp"),
        P(),
        P("dp", "tensor"),
        P("dp", "tensor"),
        P("dp", "tensor"),
        P("tensor", "dp"),
        P("tensor", "dp"),
        P("dp", None),
        P("dp", None),
        P("dp", "tensor"),
        P("dp", "tensor"),
        P("dp", "tensor", None),
        P("dp", "tensor", None),
        P("dp", "tensor", None),
    )
    return jax.shard_map(
        functools.partial(per_device, n, nt),
        mesh=mesh, in_specs=in_specs, out_specs=P("dp", "tensor", None), check_vma=False,
    )
```

time: 624 us -> 290 us (0.46)
  waiting for transfers between devices: 504 us -> 0 us
  Pallas kernels: 0 us -> 282 us
  other arithmetic: 38.4 us -> 1.46 us
  matrix products: 31.1 us -> 0 us
  between operations: 14.2 us -> 0.67 us
  starting transfers between devices: 13.2 us -> 0 us
  blocking collectives: 10.7 us -> 0 us
    all_gather x7 -> x0, waiting for transfers between devices: 447 us -> none  [the longest x1 84.6 us: per_device(): lax.all_gather(context_w, 'dp', axis=1, tiled=True)]
    pallas_call x0 -> x1, Pallas kernels: none -> 282 us  [per_device(): pl.pallas_call(functools.partial(kernel, n, nt), out_shape=jax.ShapeDtype...]
    psum x2 -> x0, waiting for transfers between devices: 46.9 us -> none  [the longest x1 46.9 us: per_device(): lax.psum(partial_value.astype(jnp.bfloat16), 'tensor').astype(jnp.float32)]
    dot_general x11 -> x0, matrix products: 31.1 us -> none  [the longest x3 10.5 us: per_device(): jnp.dot(columns, piece, preferred_element_type=jnp.float32)]
    unnamed x5 -> x2, other arithmetic: 29.2 us -> 1.46 us
    all_to_all x3 -> x0, starting transfers between devices: 12.7 us -> none  [the longest x1 5.18 us: per_device(): lax.all_to_all(image_key, 'tensor', split_axis=2, concat_axis=1, tiled=True)]
    all_to_all x1 -> x0, blocking collectives: 10.7 us -> none  [per_device(): lax.all_to_all(attended, 'tensor', split_axis=1, concat_axis=2, tiled=True)]
    reduce_sum x5 -> x0, other arithmetic: 6.63 us -> none  [the longest x2 2.74 us: masked_softmax(): return (expo, jnp.sum(expo, axis=-1, keepdims=True))]
  transfers between devices with their start and end apart: 12 -> 0, of which waited for: 10 -> 0; matrix products, arithmetic and copies ran while one was open for 9% -> 0% of each run, Pallas kernels for 0% -> 0%
where the time goes in v1:
time: 290 us
  Pallas kernels  282 us (97%)
  local copies, waits for them, and re-layouts  5.38 us (2%)
    pallas_call x1, Pallas kernels, per_device(): pl.pallas_call(functools.partial(kernel, n, nt), out_shape=jax.ShapeDtype...  282 us

profile of v1, /device:TPU:1, one launch (start us, length us, event | category | flops | bytes accessed | tf_op | source)
XLA Modules:
  0.0 289.9 jit_solution(8296217590989203293)
XLA Ops:
  0.7 0.7 reduce
  1.4 0.7 reshape.26.refs_3_
  2.1 0.7 reduce.1
  2.8 0.7 reshape.27.refs_4_
  3.5 2.2 copy.16.refs_9_
  5.7 282.4 %shard_map.145 = bf16[128,1536]{1,0:T(8,128)(2,1)} custom-call(s32[1]{0:T(128)S(6)} %copy.18.refs_0_, bf16[256,4096]{1,0:T(8,128)(2,1)} %bitcast.7, f32[1,4096]{1,0:T(1,128)} %bitcast.11, f32[8,1,304]{2,1,0:T(1,128)} %reshape.26.refs_3_, f32[8,1,304]{2,1,0:T(1,128)} %reshape.27.refs_4_, bf16[512,512]{1,0:T(8,128)(2,1)} %refs_5_.1, bf16[512,512]{1,0:T(8,128)(2,1)} %refs_6_.1, ...), custom_call_target="tpu_custom_call" | custom-call | flops 7130316800 | bytes 12582912 | tf_op jit(solution)/shard_map/pallas_call | solution.py:371
  288.2 1.8 copy.19

commit v2 on v1

--- a/solution.py
+++ b/solution.py
@@ -28,7 +28,7 @@
         out_ref,
         wq, wk, wv, wo, wc, wtk, wtv,
         normed, eq, ek, ev, mixed, part, part_in, emb, ctx, ctx_in, mod,
-        iq, ik, iv, tk, tv, att,
+        iq, ik, iv, tk, tv, att, scale, shift, probs, sums, part_top, part_sum, part_out,
         own_sem, ring_send, ring_recv, img_send, img_recv, img_own,
         part_send, part_recv, ctx_send, ctx_recv, mod_send, mod_recv,
         att_send, att_recv, att_own,
@@ -86,13 +86,21 @@
         for chunk in group:
             hop(chunk, 0).start()
 
-    def run_ring(group, first, last):
-        @pl.loop(first, last)
+    def move(group, step):
+        for chunk in group:
+            hop(chunk, step - 1, incoming=True).wait_recv()
+            hop(chunk, step - 1).wait_send()
+            hop(chunk, step).start()
+
+    def run_ring(group, first, last, tasks=()):
+        tasks = list(tasks)[: max(last - first, 0)]
+        for i, task in enumerate(tasks):
+            move(group, first + i)
+            task()
+
+        @pl.loop(first + len(tasks), last)
         def _(step):
-            for chunk in group:
-                hop(chunk, step - 1, incoming=True).wait_recv()
-                hop(chunk, step - 1).wait_send()
-                hop(chunk, step).start()
+            move(group, step)
 
     def close_ring(group):
         for chunk in group:
@@ -140,6 +148,11 @@
     for copy in own[2:]:
         copy.wait()
 
+    ccols = scale.shape[2]
+    for j in range(n):
+        scale[j] = scale_ref[:, j * ccols:(j + 1) * ccols]
+        shift[j] = shift_ref[:, j * ccols:(j + 1) * ccols]
+
     slots, enc = x_ref.shape
     length = len_ref[0]
 
@@ -159,29 +172,64 @@
             w = weight[:, :, block].reshape(enc, 256)
             result[:, block] = jnp.dot(normed[...], w, preferred_element_type=F32).astype(BF16)
 
-    run_ring(group_qk, 1, n - 1)
+    score = functools.partial(
+        lax.dot_general, dimension_numbers=(((1,), (1,)), ((), ())), preferred_element_type=F32
+    )
+
+    def head(h):
+        return slice(h * HEAD, (h + 1) * HEAD)
+
+    def await_images():
+        for a, (src, dst) in enumerate(images):
+            image_own[a].wait()
+            for peer in peers:
+                image_copy(a, src, dst, peer, peer).wait_recv()
+
+    def image_head(h):
+        keys = ik[:, :, head(h)].reshape(nt * lat, HEAD)
+        values = iv[:, :, head(h)].reshape(nt * lat, HEAD)
+        queries = iq[:, :, head(h)].reshape(nt * lat, HEAD)
+        scores = score(queries, keys) * HEAD ** (-0.5)
+        top = jnp.max(scores, axis=-1, keepdims=True)
+        expo = jnp.exp(scores - top)
+        part_top[h] = top
+        part_sum[h] = jnp.sum(expo, axis=-1, keepdims=True)
+        part_out[h] = jnp.dot(expo.astype(BF16), values, preferred_element_type=F32)
+
+    def encoder_head(h):
+        scores = score(eq[:, head(h)], ek[:, head(h)])
+        valid = lax.broadcasted_iota(jnp.int32, scores.shape, 1) < length
+        scores = jnp.where(valid, scores, -jnp.inf)
+        expo = jnp.exp(scores - jnp.max(scores, axis=-1, keepdims=True))
+        sums[h] = jnp.sum(expo, axis=-1, keepdims=True)
+        probs[h] = expo.astype(BF16)
+
+    image_heads = cols // HEAD
+    encoder_heads = width // HEAD
+    tasks = [await_images] + [functools.partial(image_head, h) for h in range(image_heads)]
+    run_ring(group_qk, 1, n - 1, tasks)
+    tasks = tasks[n - 2:]
     open_ring(group_vo)
     close_ring(group_qk)
+
+    def encoder_pair(h):
+        for one in range(h, min(h + 2, encoder_heads)):
+            encoder_head(one)
+
     project(wq, eq)
-    project(wk, ek)
-
-    run_ring(group_vo, 1, n - 1)
+    tasks = [functools.partial(project, wk, ek)] + tasks
+    tasks += [functools.partial(encoder_pair, h) for h in range(0, encoder_heads, 2)]
+    run_ring(group_vo, 1, n - 1, tasks)
+    for task in tasks[n - 2:]:
+        task()
     open_ring(group_c)
     open_ring(group_t)
     close_ring(group_vo)
     project(wv, ev)
-
-    for h in range(width // HEAD):
-        at = slice(h * HEAD, (h + 1) * HEAD)
-        scores = lax.dot_general(
-            eq[:, at], ek[:, at], (((1,), (1,)), ((), ())), preferred_element_type=F32
-        )
-        valid = lax.broadcasted_iota(jnp.int32, scores.shape, 1) < length
-        scores = jnp.where(valid, scores, -jnp.inf)
-        expo = jnp.exp(scores - jnp.max(scores, axis=-1, keepdims=True))
-        total = jnp.sum(expo, axis=-1, keepdims=True)
-        value = jnp.dot(expo.astype(BF16), ev[:, at], preferred_element_type=F32)
-        mixed[:, at] = (value / total).astype(BF16)
+    for h in range(encoder_heads):
+        value = jnp.dot(probs[h], ev[:, head(h)], preferred_element_type=F32)
+        mixed[:, head(h)] = (value / sums[h]).astype(BF16)
+    run_ring(group_c, 1, 2)
 
     ocols = o_in.shape[1]
     share = enc // nt
@@ -201,7 +249,8 @@
 
     for peer in peers:
         part_copy(peer, t).start()
-    run_ring(group_c, 1, n - 1)
+    arrive = 2 + (n - 2) // 3
+    run_ring(group_c, 2, arrive)
     for peer in peers:
         part_copy(peer, peer).wait_recv()
 
@@ -214,11 +263,13 @@
         x = x_ref[block, pl.ds(pl.multiple_of(t * share, 128), share)].astype(F32)
         emb[block, :] = (x + total).astype(BF16)
 
+    run_ring(group_c, arrive, n - 1)
+    run_ring(group_t, 1, 2)
     close_ring(group_c)
 
     @pl.loop(0, n)
     def _(j):
-        ctx[j] = jnp.dot(emb[...], wc[j], preferred_element_type=F32).astype(BF16)
+        ctx[j] = score(emb[...], wc[j]).astype(BF16)
 
     trow = slots // nt
 
@@ -234,8 +285,8 @@
 
     for peer in peers:
         ctx_copy(peer, t).start()
-    middle = 1 + (n - 1) // 3
-    run_ring(group_t, 1, middle)
+    middle = 2 + (n - 1) // 3
+    run_ring(group_t, 2, middle)
     for peer in peers:
         ctx_copy(peer, peer).wait_recv()
     context = ctx[:, token_rows(t), :].astype(F32)
@@ -248,7 +299,7 @@
 
     centered = context - mean(context)
     spread = mean(centered * centered)
-    modulated = centered * lax.rsqrt(spread + EPS) * (1.0 + scale_ref[...]) + shift_ref[...]
+    modulated = centered * lax.rsqrt(spread + EPS) * (1.0 + scale[...]) + shift[...]
     mod[:, token_rows(t), :] = modulated.astype(BF16)
 
     def mod_copy(peer, place_of):
@@ -262,10 +313,6 @@
     for peer in peers:
         mod_copy(peer, t).start()
     run_ring(group_t, middle, n - 1)
-    for a, (src, dst) in enumerate(images):
-        image_own[a].wait()
-        for peer in peers:
-            image_copy(a, src, dst, peer, peer).wait_recv()
     for peer in peers:
         mod_copy(peer, peer).wait_recv()
     close_ring(group_t)
@@ -279,27 +326,18 @@
     text_project(wtk, tk)
     text_project(wtv, tv)
 
-    for h in range(cols // HEAD):
-        at = slice(h * HEAD, (h + 1) * HEAD)
-        keys = ik[:, :, at].reshape(nt * lat, HEAD)
-        values = iv[:, :, at].reshape(nt * lat, HEAD)
-        queries = iq[:, :, at].reshape(nt * lat, HEAD)
-        score = functools.partial(
-            lax.dot_general, dimension_numbers=(((1,), (1,)), ((), ())), preferred_element_type=F32
-        )
-        first = score(queries, keys) * HEAD ** (-0.5)
-        second = score(queries, tk[:, at]) * HEAD ** (-0.5)
-        valid = lax.broadcasted_iota(jnp.int32, second.shape, 1) < length
-        second = jnp.where(valid, second, -jnp.inf)
-        top = jnp.maximum(
-            jnp.max(first, axis=-1, keepdims=True), jnp.max(second, axis=-1, keepdims=True)
-        )
-        first = jnp.exp(first - top)
-        second = jnp.exp(second - top)
-        total = jnp.sum(first, axis=-1, keepdims=True) + jnp.sum(second, axis=-1, keepdims=True)
-        value = jnp.dot(first.astype(BF16), values, preferred_element_type=F32)
-        value = value + jnp.dot(second.astype(BF16), tv[:, at], preferred_element_type=F32)
-        att[:, :, at] = (value / total).astype(BF16).reshape(nt, lat, HEAD)
+    for h in range(image_heads):
+        queries = iq[:, :, head(h)].reshape(nt * lat, HEAD)
+        scores = score(queries, tk[:, head(h)]) * HEAD ** (-0.5)
+        valid = lax.broadcasted_iota(jnp.int32, scores.shape, 1) < length
+        scores = jnp.where(valid, scores, -jnp.inf)
+        top = jnp.maximum(part_top[h], jnp.max(scores, axis=-1, keepdims=True))
+        expo = jnp.exp(scores - top)
+        shrink = jnp.exp(part_top[h] - top)
+        total = part_sum[h] * shrink + jnp.sum(expo, axis=-1, keepdims=True)
+        value = jnp.dot(expo.astype(BF16), tv[:, head(h)], preferred_element_type=F32)
+        value = part_out[h] * shrink + value
+        att[:, :, head(h)] = (value / total).astype(BF16).reshape(nt, lat, HEAD)
 
     def att_copy(peer, place_of):
         return pltpu.make_async_remote_copy(
@@ -337,7 +375,7 @@
     vmem = pl.BlockSpec(memory_space=pltpu.VMEM)
     anywhere = pl.BlockSpec(memory_space=pl.ANY)
     dma = pltpu.SemaphoreType.DMA
-    scratch = [pltpu.VMEM((n,) + w.shape, BF16) for w in (query_w, key_w, value_w, out_w, context_w, text_key_w, text_value_w)]
+    scratch = [pltpu.VMEM((n,) + w.shape, BF16) for w in (query_w, key_w, value_w, out_w, context_w.T, text_key_w, text_value_w)]
     scratch += [
         pltpu.VMEM((slots, enc), BF16),
         pltpu.VMEM((slots, width), BF16),
@@ -356,6 +394,13 @@
         pltpu.VMEM((slots, cols), BF16),
         pltpu.VMEM((slots, cols), BF16),
         pltpu.VMEM((nt, lat, cols), BF16),
+        pltpu.VMEM((n, 1, ccols), F32),
+        pltpu.VMEM((n, 1, ccols), F32),
+        pltpu.VMEM((width // HEAD, slots, slots), BF16),
+        pltpu.VMEM((width // HEAD, slots, 1), F32),
+        pltpu.VMEM((cols // HEAD, nt * lat, 1), F32),
+        pltpu.VMEM((cols // HEAD, nt * lat, 1), F32),
+        pltpu.VMEM((cols // HEAD, nt * lat, HEAD), F32),
         dma((7,)), dma((16,)), dma((16, n - 1)),
         dma((3, nt)), dma((3, nt)), dma((3,)),
         dma((nt,)), dma((nt,)), dma((nt,)), dma((nt,)), dma((nt,)), dma((nt,)),
@@ -382,9 +427,9 @@
         prompt_lengths,
         text_states.reshape(slots, enc),
         attn_gain.reshape(1, enc),
-        mod_scale.reshape(n, 1, ccols),
-        mod_shift.reshape(n, 1, ccols),
-        query_w, key_w, value_w, out_w, context_w, text_key_w, text_value_w,
+        mod_scale,
+        mod_shift,
+        query_w, key_w, value_w, out_w, context_w.T, text_key_w, text_value_w,
         laid_out(image_query), laid_out(image_key), laid_out(image_value),
     )
     if apart:

time: 290 us -> 277 us (0.955)
  Pallas kernels: 282 us -> 274 us
  local copies, waits for them, and re-layouts: 5.38 us -> 1.77 us
    pallas_call x1, Pallas kernels: 282 us -> 274 us  [per_device(): pl.pallas_call(functools.partial(kernel, n, nt), out_shape=jax.ShapeDtype...]
where the time goes in v2:
time: 277 us; the launch traced here: 276 us
  Pallas kernels  274 us (99%)
    pallas_call x1, Pallas kernels, per_device(): pl.pallas_call(functools.partial(kernel, n, nt), out_shape=jax.ShapeDtype...  274 us

profile of v2, /device:TPU:1, one launch (start us, length us, event | category | flops | bytes accessed | tf_op | source)
XLA Modules:
  0.0 276.3 jit_solution(8950992783243333573)
XLA Ops:
  0.7 273.9 %shard_map.145 = bf16[128,1536]{1,0:T(8,128)(2,1)} custom-call(s32[1]{0:T(128)S(6)} %copy.17.refs_0_, bf16[256,4096]{1,0:T(8,128)(2,1)} %bitcast.8, f32[1,4096]{1,0:T(1,128)} %bitcast.13, f32[1,2432]{1,0:T(1,128)} %refs_3_.1, f32[1,2432]{1,0:T(1,128)} %refs_4_.1, bf16[512,512]{1,0:T(8,128)(2,1)} %refs_5_.1, bf16[512,512]{1,0:T(8,128)(2,1)} %refs_6_.1, ...), custom_call_target="tpu_custom_call" | custom-call | flops 7130316800 | bytes 12582912 | tf_op jit(solution)/shard_map/pallas_call | solution.py:416
  274.6 1.8 copy.18

commit v3 on v2

--- a/solution.py
+++ b/solution.py
@@ -92,13 +92,8 @@
             hop(chunk, step - 1).wait_send()
             hop(chunk, step).start()
 
-    def run_ring(group, first, last, tasks=()):
-        tasks = list(tasks)[: max(last - first, 0)]
-        for i, task in enumerate(tasks):
-            move(group, first + i)
-            task()
-
-        @pl.loop(first + len(tasks), last)
+    def run_ring(group, first, last):
+        @pl.loop(first, last)
         def _(step):
             move(group, step)
 
@@ -206,24 +201,39 @@
 
     image_heads = cols // HEAD
     encoder_heads = width // HEAD
+    def encoder_run(first, last):
+        for h in range(first, last):
+            encoder_head(h)
+
     tasks = [await_images] + [functools.partial(image_head, h) for h in range(image_heads)]
-    run_ring(group_qk, 1, n - 1, tasks)
-    tasks = tasks[n - 2:]
+    lag = 2
+    move(group_qk, 1)
+    move(group_qk, 2)
     open_ring(group_vo)
+    for step in range(3, min(n - 1, 7)):
+        move(group_qk, step)
+        for task in tasks[:1]:
+            task()
+        move(group_vo, step - lag)
+        for task in tasks[1:2]:
+            task()
+        tasks = tasks[2:]
+    if n - 1 > 7:
+        @pl.loop(7, n - 1)
+        def _(step):
+            move(group_qk, step)
+            move(group_vo, step - lag)
+    for task in tasks:
+        task()
     close_ring(group_qk)
-
-    def encoder_pair(h):
-        for one in range(h, min(h + 2, encoder_heads)):
-            encoder_head(one)
-
     project(wq, eq)
-    tasks = [functools.partial(project, wk, ek)] + tasks
-    tasks += [functools.partial(encoder_pair, h) for h in range(0, encoder_heads, 2)]
-    run_ring(group_vo, 1, n - 1, tasks)
-    for task in tasks[n - 2:]:
-        task()
+    move(group_vo, n - 3)
+    project(wk, ek)
+    encoder_run(0, encoder_heads // 2)
+    move(group_vo, n - 2)
     open_ring(group_c)
     open_ring(group_t)
+    encoder_run(encoder_heads // 2, encoder_heads)
     close_ring(group_vo)
     project(wv, ev)
     for h in range(encoder_heads):
@@ -249,7 +259,7 @@
 
     for peer in peers:
         part_copy(peer, t).start()
-    arrive = 2 + (n - 2) // 3
+    arrive = 3 + (n - 2) // 3
     run_ring(group_c, 2, arrive)
     for peer in peers:
         part_copy(peer, peer).wait_recv()
@@ -285,7 +295,7 @@
 
     for peer in peers:
         ctx_copy(peer, t).start()
-    middle = 2 + (n - 1) // 3
+    middle = 3 + (n - 1) // 3
     run_ring(group_t, 2, middle)
     for peer in peers:
         ctx_copy(peer, peer).wait_recv()

time: 277 us -> 277 us (level)
  no operation moved by 1% of the time
where the time goes in v3:
time: 277 us
  Pallas kernels  274 us (99%)
    pallas_call x1, Pallas kernels, per_device(): pl.pallas_call(functools.partial(kernel, n, nt), out_shape=jax.ShapeDtype...  274 us

profile of v3, /device:TPU:1, one launch (start us, length us, event | category | flops | bytes accessed | tf_op | source)
XLA Modules:
  0.0 276.7 jit_solution(18426325869864608982)
XLA Ops:
  0.7 274.2 %shard_map.145 = bf16[128,1536]{1,0:T(8,128)(2,1)} custom-call(s32[1]{0:T(128)S(6)} %copy.17.refs_0_, bf16[256,4096]{1,0:T(8,128)(2,1)} %bitcast.8, f32[1,4096]{1,0:T(1,128)} %bitcast.13, f32[1,2432]{1,0:T(1,128)} %refs_3_.1, f32[1,2432]{1,0:T(1,128)} %refs_4_.1, bf16[512,512]{1,0:T(8,128)(2,1)} %refs_5_.1, bf16[512,512]{1,0:T(8,128)(2,1)} %refs_6_.1, ...), custom_call_target="tpu_custom_call" | custom-call | flops 7130316800 | bytes 12582912 | tf_op jit(solution)/shard_map/pallas_call | solution.py:426
  274.9 1.8 copy.18

commit v4 on v3

--- a/solution.py
+++ b/solution.py
@@ -336,19 +336,6 @@
     text_project(wtk, tk)
     text_project(wtv, tv)
 
-    for h in range(image_heads):
-        queries = iq[:, :, head(h)].reshape(nt * lat, HEAD)
-        scores = score(queries, tk[:, head(h)]) * HEAD ** (-0.5)
-        valid = lax.broadcasted_iota(jnp.int32, scores.shape, 1) < length
-        scores = jnp.where(valid, scores, -jnp.inf)
-        top = jnp.maximum(part_top[h], jnp.max(scores, axis=-1, keepdims=True))
-        expo = jnp.exp(scores - top)
-        shrink = jnp.exp(part_top[h] - top)
-        total = part_sum[h] * shrink + jnp.sum(expo, axis=-1, keepdims=True)
-        value = jnp.dot(expo.astype(BF16), tv[:, head(h)], preferred_element_type=F32)
-        value = part_out[h] * shrink + value
-        att[:, :, head(h)] = (value / total).astype(BF16).reshape(nt, lat, HEAD)
-
     def att_copy(peer, place_of):
         return pltpu.make_async_remote_copy(
             src_ref=att.at[peer], dst_ref=columns_of(out_ref, place_of),
@@ -356,8 +343,22 @@
             device_id=(d, peer), device_id_type=MESH,
         )
 
-    for peer in peers:
-        att_copy(peer, t).start()
+    for who in peers + [t]:
+        block = pl.ds(pl.multiple_of(who * lat, 16), lat)
+        for h in range(image_heads):
+            scores = score(iq[who, :, head(h)], tk[:, head(h)]) * HEAD ** (-0.5)
+            valid = lax.broadcasted_iota(jnp.int32, scores.shape, 1) < length
+            scores = jnp.where(valid, scores, -jnp.inf)
+            before = part_top[h, block, :]
+            top = jnp.maximum(before, jnp.max(scores, axis=-1, keepdims=True))
+            expo = jnp.exp(scores - top)
+            shrink = jnp.exp(before - top)
+            total = part_sum[h, block, :] * shrink + jnp.sum(expo, axis=-1, keepdims=True)
+            value = jnp.dot(expo.astype(BF16), tv[:, head(h)], preferred_element_type=F32)
+            value = part_out[h, block, :] * shrink + value
+            att[who, :, head(h)] = (value / total).astype(BF16)
+        if who is not t:
+            att_copy(who, t).start()
     copy = pltpu.make_async_copy(att.at[t], columns_of(out_ref, t), att_own)
     copy.start()
     copy.wait()

time: 277 us -> 275 us (level)
  no operation moved by 1% of the time
where the time goes in v4:
time: 275 us
  Pallas kernels  273 us (99%)
    pallas_call x1, Pallas kernels, per_device(): pl.pallas_call(functools.partial(kernel, n, nt), out_shape=jax.ShapeDtype...  273 us

profile of v4, /device:TPU:1, one launch (start us, length us, event | category | flops | bytes accessed | tf_op | source)
XLA Modules:
  0.0 275.2 jit_solution(2625082732212091843)
XLA Ops:
  0.7 272.7 %shard_map.145 = bf16[128,1536]{1,0:T(8,128)(2,1)} custom-call(s32[1]{0:T(128)S(6)} %copy.17.refs_0_, bf16[256,4096]{1,0:T(8,128)(2,1)} %bitcast.8, f32[1,4096]{1,0:T(1,128)} %bitcast.13, f32[1,2432]{1,0:T(1,128)} %refs_3_.1, f32[1,2432]{1,0:T(1,128)} %refs_4_.1, bf16[512,512]{1,0:T(8,128)(2,1)} %refs_5_.1, bf16[512,512]{1,0:T(8,128)(2,1)} %refs_6_.1, ...), custom_call_target="tpu_custom_call" | custom-call | flops 7130316800 | bytes 12582912 | tf_op jit(solution)/shard_map/pallas_call | solution.py:427
  273.4 1.8 copy.18
